TPU v7x, 32 devices: a whole 2x2x4 slice. The times are simulated.
32 devices in a mesh: row: 8 (over y, x, core), col: 4 (over z).
Axes of the slice: x: 2, y: 2, z: 4, core: 2. Of those that a mesh axis runs over, the one named last changes fastest.
Arguments:
- matrix: float32 [4096, 4096], P('row', 'col'), may hold values from -50 to 50
- panel_index: int32 [1], replicated, may hold values from 0 to 14
Outputs:
- factored: float32 [4096, 4096], P('row', 'col')
All inputs are finite; a program needn't handle non-finite values.
Results may differ from a plain program's by a relative error of at most 0.0003.
Values sent between devices are 32-bit elements; how exact they have to be, the bound alone decides.
A program may use at most 64 MiB of HBM per device.

v0:
```python
import jax
import jax.numpy as jnp
from jax import lax
from jax.sharding import PartitionSpec as P

NB = 128
STEPS = 2


HIGHEST_PRECISION = lax.Precision.HIGHEST


def broadcast(shard, axis, root):
    mine = lax.axis_index(axis) == root
    return lax.psum(jnp.where(mine, shard, jnp.zeros_like(shard)), axis)


def place_row(target_matrix, new_row, row_number, positions):
    return target_matrix + new_row[None, :] * (positions[:, None] == row_number).astype(jnp.float32)


def lower_cholesky(gram_total):
    order_size = gram_total.shape[0]
    positions = jnp.arange(order_size, dtype=jnp.int32)

    def column_step(column_number, carry):
        working, lower_tri = carry
        column = lax.dynamic_index_in_dim(working, column_number, 1, keepdims=False)
        pivot = lax.dynamic_index_in_dim(column, column_number, 0, keepdims=False)
        scaled = jnp.where(positions >= column_number, column / jnp.sqrt(pivot), 0.0)
        working = working - scaled[:, None] * scaled[None, :]
        lower_tri = lower_tri + scaled[:, None] * (positions[None, :] == column_number).astype(
            jnp.float32
        )
        return (working, lower_tri)

    start = (gram_total, jnp.zeros_like(gram_total))
    return lax.fori_loop(0, order_size, column_step, start)[1]


def upper_inverse(upper_tri):
    order_size = upper_tri.shape[0]
    positions = jnp.arange(order_size, dtype=jnp.int32)

    def upper_row_step(counter, solved):
        row_number = order_size - 1 - counter
        full_row = lax.dynamic_index_in_dim(upper_tri, row_number, 0, keepdims=False)
        pivot = lax.dynamic_index_in_dim(full_row, row_number, 0, keepdims=False)
        off_part = jnp.where(positions > row_number, full_row, 0.0)
        unit_row = (positions == row_number).astype(jnp.float32)
        new_row = (unit_row - jnp.sum(off_part[:, None] * solved, axis=0)) / pivot
        return place_row(solved, new_row, row_number, positions)

    return lax.fori_loop(0, order_size, upper_row_step, jnp.zeros_like(upper_tri))


def unit_lower_solve(lower_unit, right_side):
    order_size = lower_unit.shape[0]
    positions = jnp.arange(order_size, dtype=jnp.int32)

    def unit_row_step(row_number, solved):
        full_row = lax.dynamic_index_in_dim(lower_unit, row_number, 0, keepdims=False)
        off_part = jnp.where(positions < row_number, full_row, 0.0)
        given_row = lax.dynamic_index_in_dim(right_side, row_number, 0, keepdims=False)
        new_row = given_row - jnp.sum(off_part[:, None] * solved, axis=0)
        return place_row(solved, new_row, row_number, positions)

    return lax.fori_loop(0, order_size, unit_row_step, jnp.zeros_like(right_side))


def triangular_split(square):
    order_size = square.shape[0]
    positions = jnp.arange(order_size, dtype=jnp.int32)
    identity = jnp.eye(order_size, dtype=jnp.float32)

    def eliminate(column_number, carry):
        remaining, lower_unit = carry
        pivot_row = lax.dynamic_index_in_dim(remaining, column_number, 0, keepdims=False)
        pivot_value = lax.dynamic_index_in_dim(pivot_row, column_number, 0, keepdims=False)
        column = lax.dynamic_index_in_dim(remaining, column_number, 1, keepdims=False)
        multiplier = jnp.where(positions > column_number, column / pivot_value, 0.0)
        remaining = remaining - multiplier[:, None] * pivot_row[None, :]
        lower_unit = lower_unit + multiplier[:, None] * (
            positions[None, :] == column_number
        ).astype(jnp.float32)
        return (remaining, lower_unit)

    remaining, lower_unit = lax.fori_loop(0, order_size, eliminate, (square, identity))
    return (lower_unit, jnp.triu(remaining))


def upper_factor(gram_total):
    identity = jnp.eye(gram_total.shape[0], dtype=jnp.float32)
    is_empty = jnp.trace(gram_total) <= 0.0
    lower_tri = lower_cholesky(gram_total + jnp.where(is_empty, 1.0, 0.0) * identity)
    return jnp.where(is_empty, jnp.zeros_like(lower_tri), lower_tri.T)


def per_device(matrix, panel_index):
    row_count, col_count = matrix.shape
    col_devices = lax.axis_size("col")
    my_row = lax.axis_index("row")
    my_col = lax.axis_index("col")
    global_row = my_row * row_count + jnp.arange(row_count, dtype=jnp.int32)
    column_block = jnp.arange(col_count, dtype=jnp.int32) // NB * col_devices + my_col
    identity = jnp.eye(NB, dtype=jnp.float32)
    diag_index = jnp.arange(NB, dtype=jnp.int32)
    current = matrix
    for section_index in range(STEPS):
        target = panel_index[0] + section_index
        owner_col = target % col_devices
        local_start = target // col_devices * NB
        first_row = target * NB
        top_device = first_row // row_count
        top_offset = first_row % row_count
        active = global_row >= first_row
        initial = lax.dynamic_slice_in_dim(current, local_start, NB, 1)
        panel_block = jnp.where(active[:, None], initial, 0.0)
        top_slice = lax.dynamic_slice_in_dim(panel_block, top_offset, NB, 0)
        gram_local = jnp.einsum("ri,rj->ij", panel_block, panel_block, precision=HIGHEST_PRECISION)
        top_local = jnp.where(my_row == top_device, top_slice, 0.0)
        gram_total, top_block = lax.psum((gram_local, top_local), "row")
        tri_factor = upper_factor(gram_total)
        factor_inv = upper_inverse(tri_factor)
        ortho_local = jnp.dot(panel_block, factor_inv, precision=HIGHEST_PRECISION)
        ortho_top = jnp.dot(top_block, factor_inv, precision=HIGHEST_PRECISION)
        lower_unit, upper_tri = triangular_split(ortho_top + identity)
        upper_inv = upper_inverse(upper_tri)
        shift_rows = ((global_row - first_row)[:, None] == diag_index[None, :]).astype(jnp.float32)
        reflect = jnp.dot(ortho_local + shift_rows, upper_inv, precision=HIGHEST_PRECISION)
        reflect = jnp.where(active[:, None], reflect, 0.0)
        t_transposed = unit_lower_solve(lower_unit, upper_tri.T)
        reflect, t_transposed = (
            broadcast(reflect, "col", owner_col),
            broadcast(t_transposed, "col", owner_col),
        )
        trailing = column_block > target
        projection = lax.psum(
            jnp.einsum("rc,rk->ck", current, reflect, precision=HIGHEST_PRECISION), "row"
        )
        coefficients = jnp.einsum(
            "ck,jk->cj", projection, t_transposed, precision=HIGHEST_PRECISION
        )
        count_cols = coefficients.shape[0]
        columns = lax.slice_in_dim(current, 0, count_cols, axis=1)
        keep_mask = lax.slice_in_dim(trailing, 0, count_cols, axis=0)
        change = jnp.einsum("rk,ck->rc", reflect, coefficients, precision=HIGHEST_PRECISION)
        updated = jnp.where(keep_mask[None, :], columns - change, columns)
        new_panel = jnp.where(active[:, None], reflect, initial)
        written = lax.dynamic_update_slice_in_dim(updated, new_panel, local_start, 1)
        current = jnp.where(my_col == owner_col, written, updated)
    return current


def solution(mesh):
    return jax.shard_map(
        per_device,
        mesh=mesh,
        in_specs=(P("row", "col"), P()),
        out_specs=P("row", "col"),
        check_vma=False,
    )
```

profile of v0, /device:TPU:0, one launch (start us, length us, event | category | flops | bytes accessed | tf_op | source)
XLA Modules:
  0.0 1950.6 jit_solution(15672030127321959402)
XLA Ops:
  7.3 1.1 dynamic-slice_select_fusion.1
  8.4 1.2 fusion.42
  10.5 55.7 %all-reduce.17.cloned.1.call-done = (f32[128,128]{1,0:T(8,128)}, f32[128,128]{1,0:T(8,128)}) async-done(((f32[128,128]{1,0:T(8,128)}, f32[128,128]{1,0:T(8,128)}), (f32[128,128]{1,0:T(8,128)}, f32[128,128]{1,0:T(8,128)})) %all-reduce.17.cloned.1.call-update) | async-done | bytes 131088 | tf_op jit(solution)/shard_map/psum | solution.py:122
  66.2 1.5 select_reduce_fusion.1
  68.3 0.9 select_add_fusion.3
  69.3 187.6 %while.184 = (s32[]{:T(128)}, f32[128,128]{0,1:T(8,128)S(1)}, f32[128,128]{0,1:T(8,128)S(1)}, s32[]{:T(128)}, s32[]{:T(128)}, /*index=5*/s32[]{:T(128)}) while((s32[]{:T(128)}, f32[128,128]{0,1:T(8,128)S(1)}, f32[128,128]{0,1:T(8,128)S(1)}, s32[]{:T(128)}, s32[]{:T(128)}, /*index=5*/s32[]{:T(128)}) %tuple.425), condition=%wide.region_3.4_spmd.clone.clone, body=%wide.region_2.3_spmd.clone.clone.sunk | while | flops 82820 | bytes 267911 | solution.py:38
  257.1 190.6 %while.185 = (s32[]{:T(128)}, f32[128,128]{1,0:T(8,128)S(1)}, f32[128,128]{1,0:T(8,128)S(1)}, s32[]{:T(128)}, s32[]{:T(128)}, /*index=5*/s32[]{:T(128)}, s32[]{:T(128)}) while((s32[]{:T(128)}, f32[128,128]{1,0:T(8,128)S(1)}, f32[128,128]{1,0:T(8,128)S(1)}, s32[]{:T(128)}, s32[]{:T(128)}, /*index=5*/s32[]{:T(128)}, ...), condition=%wide.region_6.7_spmd.clone.clone, body=%wide.region_4.6_spmd.clone.clone.sunk | while | flops 99208 | bytes 201406 | solution.py:54
  266.7 0.7 subtract_divide_fusion.8
  283.1 0.7 subtract_divide_fusion.8
  295.0 0.7 subtract_divide_fusion.8
  311.4 0.7 subtract_divide_fusion.8
  323.3 0.7 subtract_divide_fusion.8
  339.7 0.7 subtract_divide_fusion.8
  351.6 0.7 subtract_divide_fusion.8
  368.0 0.7 subtract_divide_fusion.8
  379.9 0.7 subtract_divide_fusion.8
  396.2 0.7 subtract_divide_fusion.8
  408.2 0.7 subtract_divide_fusion.8
  424.5 0.7 subtract_divide_fusion.8
  436.4 0.7 subtract_divide_fusion.8
  448.0 202.9 %while.182 = (s32[]{:T(128)}, f32[128,128]{0,1:T(8,128)S(1)}, f32[128,128]{0,1:T(8,128)S(1)}, s32[]{:T(128)}, s32[]{:T(128)}, /*index=5*/s32[]{:T(128)}) while((s32[]{:T(128)}, f32[128,128]{0,1:T(8,128)S(1)}, f32[128,128]{0,1:T(8,128)S(1)}, s32[]{:T(128)}, s32[]{:T(128)}, /*index=5*/s32[]{:T(128)}) %tuple.431), condition=%wide.region_9.10_spmd.clone.clone, body=%wide.region_8.9_spmd.clone.clone.sunk | while | flops 66179 | bytes 267381 | solution.py:88
  651.7 32.5 %while.187 = (s32[]{:T(128)}, f32[128,128]{1,0:T(8,128)S(1)}, f32[128,128]{1,0:T(8,128)S(1)}, f32[128,128]{1,0:T(8,128)S(1)}, s32[]{:T(128)}, /*index=5*/s32[]{:T(128)}) while((s32[]{:T(128)}, f32[128,128]{1,0:T(8,128)S(1)}, f32[128,128]{1,0:T(8,128)S(1)}, f32[128,128]{1,0:T(8,128)S(1)}, s32[]{:T(128)}, ...), condition=%wide.region_17.18_spmd.clone.clone, body=%wide.region_15.17_spmd.clone.clone.sunk | while | flops 98819 | bytes 202848 | solution.py:68
  684.2 190.6 %while.186 = (s32[]{:T(128)}, f32[128,128]{1,0:T(8,128)S(1)}, f32[128,128]{1,0:T(8,128)S(1)}, s32[]{:T(128)}, s32[]{:T(128)}, /*index=5*/s32[]{:T(128)}, s32[]{:T(128)}) while((s32[]{:T(128)}, f32[128,128]{1,0:T(8,128)S(1)}, f32[128,128]{1,0:T(8,128)S(1)}, s32[]{:T(128)}, s32[]{:T(128)}, /*index=5*/s32[]{:T(128)}, ...), condition=%wide.region_12.13_spmd.clone.clone, body=%wide.region_10.12_spmd.clone.clone.sunk | while | flops 99208 | bytes 201406 | solution.py:54
  692.4 0.7 subtract_divide_fusion.9
  708.8 0.7 subtract_divide_fusion.9
  875.4 1.1 fusion.27
  876.6 35.8 %all-reduce.21.cloned.1.call-done = (f32[512,128]{1,0:T(8,128)}, f32[128,128]{1,0:T(8,128)}) async-done(((f32[512,128]{1,0:T(8,128)}, f32[128,128]{1,0:T(8,128)}), (f32[512,128]{1,0:T(8,128)}, f32[128,128]{1,0:T(8,128)})) %all-reduce.21.cloned.1.call-update) | async-done | bytes 327696 | tf_op jit(solution)/shard_map/psum | solution.py:15
  912.4 3.1 convolution_bitcast_fusion
  915.7 54.4 %all-reduce.11.cloned.1.call-done = f32[1024,128]{0,1:T(8,128)} async-done(((f32[1024,128]{0,1:T(8,128)}), f32[1024,128]{0,1:T(8,128)}) %all-reduce.11.cloned.1.call-update) | async-done | bytes 524304 | tf_op jit(solution)/shard_map/psum | solution.py:138
  970.1 2.0 fusion.43
  972.2 3.4 subtract_select_fusion.1
  975.6 1.1 select_dynamic-update-slice_fusion.1
  976.9 1.2 fusion.44
  978.8 52.4 %all-reduce.15.cloned.1.call-done = (f32[128,128]{1,0:T(8,128)}, f32[128,128]{1,0:T(8,128)}) async-done(((f32[128,128]{1,0:T(8,128)}, f32[128,128]{1,0:T(8,128)}), (f32[128,128]{1,0:T(8,128)}, f32[128,128]{1,0:T(8,128)})) %all-reduce.15.cloned.1.call-update) | async-done | bytes 131088 | tf_op jit(solution)/shard_map/psum | solution.py:122
  1031.2 1.5 select_reduce_fusion
  1033.4 0.9 select_add_fusion.2
  1034.3 187.6 %while.188 = (s32[]{:T(128)}, f32[128,128]{0,1:T(8,128)S(1)}, f32[128,128]{0,1:T(8,128)S(1)}, s32[]{:T(128)}, s32[]{:T(128)}, /*index=5*/s32[]{:T(128)}) while((s32[]{:T(128)}, f32[128,128]{0,1:T(8,128)S(1)}, f32[128,128]{0,1:T(8,128)S(1)}, s32[]{:T(128)}, s32[]{:T(128)}, /*index=5*/s32[]{:T(128)}) %tuple.440), condition=%wide.region_22.23_spmd.clone.clone, body=%wide.region_21.22_spmd.clone.clone.sunk | while | flops 82820 | bytes 267911 | solution.py:38
  1222.1 190.6 %while.189 = (s32[]{:T(128)}, f32[128,128]{1,0:T(8,128)S(1)}, f32[128,128]{1,0:T(8,128)S(1)}, s32[]{:T(128)}, s32[]{:T(128)}, /*index=5*/s32[]{:T(128)}, s32[]{:T(128)}) while((s32[]{:T(128)}, f32[128,128]{1,0:T(8,128)S(1)}, f32[128,128]{1,0:T(8,128)S(1)}, s32[]{:T(128)}, s32[]{:T(128)}, /*index=5*/s32[]{:T(128)}, ...), condition=%wide.region_25.26_spmd.clone.clone, body=%wide.region_23.25_spmd.clone.clone.sunk | while | flops 99208 | bytes 201406 | solution.py:54
  1413.0 202.9 %while.183 = (s32[]{:T(128)}, f32[128,128]{0,1:T(8,128)S(1)}, f32[128,128]{0,1:T(8,128)S(1)}, s32[]{:T(128)}, s32[]{:T(128)}, /*index=5*/s32[]{:T(128)}) while((s32[]{:T(128)}, f32[128,128]{0,1:T(8,128)S(1)}, f32[128,128]{0,1:T(8,128)S(1)}, s32[]{:T(128)}, s32[]{:T(128)}, /*index=5*/s32[]{:T(128)}) %tuple.446), condition=%wide.region_28.29_spmd.clone.clone, body=%wide.region_27.28_spmd.clone.clone.sunk | while | flops 66179 | bytes 267381 | solution.py:88
  1616.8 32.5 %while.191 = (s32[]{:T(128)}, f32[128,128]{1,0:T(8,128)S(1)}, f32[128,128]{1,0:T(8,128)S(1)}, f32[128,128]{1,0:T(8,128)S(1)}, s32[]{:T(128)}, /*index=5*/s32[]{:T(128)}) while((s32[]{:T(128)}, f32[128,128]{1,0:T(8,128)S(1)}, f32[128,128]{1,0:T(8,128)S(1)}, f32[128,128]{1,0:T(8,128)S(1)}, s32[]{:T(128)}, ...), condition=%wide.region_36.37_spmd.clone.clone, body=%wide.region_34.36_spmd.clone.clone.sunk | while | flops 98819 | bytes 202848 | solution.py:68
  1649.3 190.6 %while.190 = (s32[]{:T(128)}, f32[128,128]{1,0:T(8,128)S(1)}, f32[128,128]{1,0:T(8,128)S(1)}, s32[]{:T(128)}, s32[]{:T(128)}, /*index=5*/s32[]{:T(128)}, s32[]{:T(128)}) while((s32[]{:T(128)}, f32[128,128]{1,0:T(8,128)S(1)}, f32[128,128]{1,0:T(8,128)S(1)}, s32[]{:T(128)}, s32[]{:T(128)}, /*index=5*/s32[]{:T(128)}, ...), condition=%wide.region_31.32_spmd.clone.clone, body=%wide.region_29.31_spmd.clone.clone.sunk | while | flops 99208 | bytes 201406 | solution.py:54
  1840.5 1.1 fusion.26
  1841.8 35.6 %all-reduce.19.cloned.1.call-done = (f32[512,128]{1,0:T(8,128)}, f32[128,128]{1,0:T(8,128)}) async-done(((f32[512,128]{1,0:T(8,128)}, f32[128,128]{1,0:T(8,128)}), (f32[512,128]{1,0:T(8,128)}, f32[128,128]{1,0:T(8,128)})) %all-reduce.19.cloned.1.call-update) | async-done | bytes 327696 | tf_op jit(solution)/shard_map/psum | solution.py:15
  1877.4 5.2 fusion.45
  1882.7 54.5 %all-reduce.13.cloned.1.call-done = f32[1024,128]{1,0:T(8,128)} async-done(((f32[1024,128]{1,0:T(8,128)}), f32[1024,128]{1,0:T(8,128)}) %all-reduce.13.cloned.1.call-update) | async-done | bytes 524304 | tf_op jit(solution)/shard_map/psum | solution.py:138
  1937.2 1.6 fusion.46
  1938.8 3.2 subtract_select_fusion
  1942.0 1.8 select_dynamic-update-slice_fusion
  (6970 shorter events, 1364.0 us)
Async XLA Ops:
  6.5 59.6 %all-reduce.17.cloned.1.call-start = ((), (), s32[]{:S(2)}) async-start(), calls=%async_computation.3 | async-start | bytes 262144 | tf_op jit(solution)/shard_map/psum | solution.py:122
  10.2 902.1 %all-reduce.21.cloned.1.call-start = ((), (), s32[]{:S(2)}) async-start(), calls=%async_computation.5 | async-start | bytes 655360 | tf_op jit(solution)/shard_map/psum | solution.py:15
  66.2 381.5 %copy-start.3 = (f32[128,128]{1,0:T(8,128)S(1)}, f32[128,128]{1,0:T(8,128)}, u32[]{:S(2)}) copy-start(f32[128,128]{1,0:T(8,128)} %get-tuple-element.1618) | copy-start | bytes 196612
  651.2 261.2 %copy-start = (f32[512,1024]{1,0:T(8,128)S(1)}, f32[512,1024]{1,0:T(8,128)}, u32[]{:S(2)}) copy-start(f32[512,1024]{1,0:T(8,128)} %param.22) | copy-start | bytes 6291460
  876.5 93.6 %all-reduce.11.cloned.1.call-start = ((), (), s32[]{:S(2)}) async-start(), calls=%async_computation | async-start | bytes 1048576 | tf_op jit(solution)/shard_map/psum | solution.py:138
  912.4 57.8 %copy-start.5 = (f32[128,128]{1,0:T(8,128)S(1)}, f32[128,128]{1,0:T(8,128)}, u32[]{:S(2)}) copy-start(f32[128,128]{1,0:T(8,128)} %get-tuple-element.1622) | copy-start | bytes 196612
  912.4 59.8 %copy-start.1 = (f32[512,128]{1,0:T(8,128)S(1)}, f32[512,128]{1,0:T(8,128)}, u32[]{:S(2)}) copy-start(f32[512,128]{1,0:T(8,128)} %get-tuple-element.1621) | copy-start | bytes 786436
  915.5 115.7 %all-reduce.15.cloned.1.call-start = ((), (), s32[]{:S(2)}) async-start(), calls=%async_computation.2 | async-start | bytes 262144 | tf_op jit(solution)/shard_map/psum | solution.py:122
  978.7 898.7 %all-reduce.19.cloned.1.call-start = ((), (), s32[]{:S(2)}) async-start(), calls=%async_computation.4 | async-start | bytes 655360 | tf_op jit(solution)/shard_map/psum | solution.py:15
  1031.2 381.5 %copy-start.4 = (f32[128,128]{1,0:T(8,128)S(1)}, f32[128,128]{1,0:T(8,128)}, u32[]{:S(2)}) copy-start(f32[128,128]{1,0:T(8,128)} %get-tuple-element.1616) | copy-start | bytes 196612
  1841.6 95.6 %all-reduce.13.cloned.1.call-start = ((), (), s32[]{:S(2)}) async-start(), calls=%async_computation.1 | async-start | bytes 1048576 | tf_op jit(solution)/shard_map/psum | solution.py:138
  1877.4 59.7 %copy-start.6 = (f32[128,128]{1,0:T(8,128)S(1)}, f32[128,128]{1,0:T(8,128)}, u32[]{:S(2)}) copy-start(f32[128,128]{1,0:T(8,128)} %get-tuple-element.1620) | copy-start | bytes 196612
  1877.4 61.4 %copy-start.2 = (f32[512,128]{1,0:T(8,128)S(1)}, f32[512,128]{1,0:T(8,128)}, u32[]{:S(2)}) copy-start(f32[512,128]{1,0:T(8,128)} %get-tuple-element.1619) | copy-start | bytes 786436
Sparse Core Ops, SparseCore 0:
  10.4 55.6 all-reduce.16
  876.6 35.6 all-reduce.20
  915.8 54.3 all-reduce.10
  978.9 52.3 all-reduce.14
  1841.7 35.6 all-reduce.18
  1882.8 54.3 all-reduce.12
where the time goes:
time: 1960 us; the launch traced here: 1950 us
  other arithmetic  732 us (37%)
  local copies, waits for them, and re-layouts  649 us (33%)
  waiting for transfers between devices  288 us (15%)
  loops' own time  240 us (12%)
  matrix products  24.3 us (1%)
    div x512, other arithmetic, upper_row_step(): new_row = (unit_row - jnp.sum(off_part[:, None] * solved, axis=0)) / pivot  336 us
    dynamic_slice x512, local copies, waits for them, and re-layouts, upper_row_step(): pivot = lax.dynamic_index_in_dim(full_row, row_number, 0, keepdims=False)  301 us
    another operation x2, loops' own time, lower_cholesky(): return lax.fori_loop(0, order_size, column_step, start)[1]  190 us
    mul x256, other arithmetic, eliminate(): remaining = remaining - multiplier[:, None] * pivot_row[None, :]  167 us
    dynamic_slice x256, local copies, waits for them, and re-layouts, column_step(): pivot = lax.dynamic_index_in_dim(column, column_number, 0, keepdims=False)  151 us
    dynamic_slice x256, local copies, waits for them, and re-layouts, eliminate(): lax.dynamic_index_in_dim(pivot_row, column_number, 0, keepdims=False)  151 us
    psum x2, waiting for transfers between devices, per_device(): lax.psum(jnp.einsum('rc,rk->ck', current, reflect, precision=HIGHEST_PREC...  109 us
    psum x2, waiting for transfers between devices, per_device(): gram_total, top_block = lax.psum((gram_local, top_local), 'row')  108 us

commit v1 on v0

v1 whole, which is shorter than its diff:
```python
import jax
import jax.numpy as jnp
from jax import lax
from jax.experimental import pallas as pl
from jax.experimental.pallas import tpu as pltpu
from jax.sharding import PartitionSpec as P

NB = 128
SUB = 32
HI = lax.Precision.HIGHEST


def mm(a, b, ca=1, cb=0):
    return lax.dot_general(
        a, b, (((ca,), (cb,)), ((), ())), precision=HI, preferred_element_type=jnp.float32
    )


def eliminate(chains, m_ref, n_ref):
    count = len(chains)
    rows = lax.broadcasted_iota(jnp.int32, (NB, NB), 0)
    cols = lax.broadcasted_iota(jnp.int32, (NB, NB), 1)
    unit = (rows == cols).astype(jnp.float32)
    sub_row = lax.broadcasted_iota(jnp.int32, (SUB, 1), 0)
    for i, a in enumerate(chains):
        m_ref[i] = a
        n_ref[i] = unit
    pivots = [[] for _ in chains]
    for start in range(0, NB, SUB):
        m = [m_ref[i, start : start + SUB, :] for i in range(count)]
        n = [n_ref[i, start : start + SUB, :] for i in range(count)]
        inv = [jnp.zeros((SUB, 1), jnp.float32) for _ in range(count)]
        for j in range(SUB):
            c = start + j
            for i in range(count):
                recip = 1.0 / m[i][j : j + 1, c : c + 1]
                inv[i] = jnp.where(sub_row == j, recip, inv[i])
                if j < SUB - 1:
                    mult = jnp.where(sub_row > j, m[i][:, c : c + 1] * recip, 0.0)
                    m[i] = m[i] - mult * m[i][j : j + 1, :]
                    n[i] = n[i] - mult * n[i][j : j + 1, :]
        for i in range(count):
            n_ref[i, start : start + SUB, :] = n[i]
            pivots[i].append(inv[i])
        rest = start + SUB
        if rest < NB:
            for i in range(count):
                other = m[count - 1 - i] * inv[count - 1 - i]
                both = jnp.concatenate([m[i], n[i]], axis=1)
                change = mm(other, both, 0, 0)
                m_ref[i, rest:, :] -= change[rest:, :NB]
                n_ref[i, rest:, :] -= change[rest:, NB:]
    return [jnp.concatenate(p, axis=0) for p in pivots]


def factor_panel(gram, top, m_ref, n_ref):
    rows = lax.broadcasted_iota(jnp.int32, (NB, NB), 0)
    cols = lax.broadcasted_iota(jnp.int32, (NB, NB), 1)
    unit = (rows == cols).astype(jnp.float32)
    (inv,) = eliminate([gram], m_ref, n_ref)
    w = n_ref[0] * jnp.sqrt(inv)
    b = mm(top, w, 1, 1) + unit
    _, inv_t = eliminate([b, b.T], m_ref, n_ref)
    v = n_ref[1] * inv_t
    k = mm(v, n_ref[0], 0, 0)
    return w, b, k, v


def factor_kernel(small_ref, out_ref, m_ref, n_ref):
    g11 = small_ref[0:NB, 0:NB]
    g12 = small_ref[0:NB, NB:]
    g22 = small_ref[NB : 2 * NB, NB:]
    t11 = small_ref[2 * NB : 3 * NB, 0:NB]
    t12 = small_ref[2 * NB : 3 * NB, NB:]
    t21 = small_ref[3 * NB :, 0:NB]
    t22 = small_ref[3 * NB :, NB:]
    w1, b1, k1, v1 = factor_panel(g11 + mm(t11, t11, 0, 0), t11, m_ref, n_ref)
    x12 = mm(k1, mm(w1, g12) + mm(b1, t12, 0, 0))
    z = mm(w1, x12, 0, 0)
    g11z = mm(g11, z)
    zg = mm(z, g12, 0, 0)
    gram2 = g22 - zg - zg.T + mm(z, g11z, 0, 0)
    w2, b2, k2, v2 = factor_panel(gram2, t22 - mm(t21, z), m_ref, n_ref)
    for i, a in enumerate((w1, b1, k1, v1, z, w2, k2, v2, g12 - g11z, t21)):
        out_ref[i] = a


def finish_kernel(s_ref, c_ref, a_ref, bulk_ref, fac_ref, out_ref):
    row_off = s_ref[0]
    place1, place2, target, my_col, col_devices = s_ref[1], s_ref[2], s_ref[3], s_ref[4], s_ref[5]
    height, width = c_ref.shape
    rel = lax.broadcasted_iota(jnp.int32, (height, NB), 0) + row_off
    diag = lax.broadcasted_iota(jnp.int32, (height, NB), 1)
    w1, b1, k1, v1, z, w2, k2, v2, h, t21 = [fac_ref[i] for i in range(10)]
    p1 = jnp.where(rel >= 0, a_ref[:, 0:NB], 0.0)
    full1 = mm(p1, w1, 1, 1) + (rel == diag).astype(jnp.float32)
    p2 = jnp.where(rel >= NB, a_ref[:, NB:] - mm(p1, z), 0.0)
    full2 = mm(p2, w2, 1, 1) + (rel == diag + NB).astype(jnp.float32)
    y1 = mm(full1, v1, 1, 1)
    y2 = mm(full2, v2, 1, 1)
    both = jnp.concatenate([full1, full2], axis=1)
    step = 2 * NB

    def column(i, _):
        at = pl.ds(pl.multiple_of(i * step, step), step)
        s1 = bulk_ref[0:NB, at]
        s2 = bulk_ref[NB : 2 * NB, at]
        top1 = bulk_ref[2 * NB : 3 * NB, at]
        top2 = bulk_ref[3 * NB :, at]
        block = (
            lax.broadcasted_iota(jnp.int32, (NB, step), 1) // NB + i * (step // NB)
        ) * col_devices + my_col
        x1 = mm(k1, mm(w1, s1) + mm(b1, top1, 0, 0))
        u1 = mm(w1, x1, 0, 0)
        x2 = mm(w2, s2 - mm(z, s1, 0, 0) - mm(h, u1, 0, 0)) + top2 - mm(t21, u1)
        x2 = mm(k2, x2)
        x1 = jnp.where(block > target, x1, 0.0)
        x2 = jnp.where(block > target + 1, x2, 0.0)
        out_ref[:, at] = c_ref[:, at] - mm(both, jnp.concatenate([x1, x2], axis=0))
        return 0

    lax.fori_loop(0, width // step, column, 0)

    @pl.when(place1 >= 0)
    def _():
        at = pl.ds(pl.multiple_of(place1 * NB, NB), NB)
        out_ref[:, at] = jnp.where(rel >= 0, y1, out_ref[:, at])

    @pl.when(place2 >= 0)
    def _():
        at = pl.ds(pl.multiple_of(place2 * NB, NB), NB)
        out_ref[:, at] = jnp.where(rel >= NB, y2, out_ref[:, at])


def per_device(matrix, panel_index):
    height, width = matrix.shape
    col_devices = lax.axis_size("col")
    my_row = lax.axis_index("row")
    my_col = lax.axis_index("col")
    target = panel_index[0]
    first = target * NB
    second = first + NB
    global_row = my_row * height + jnp.arange(height, dtype=jnp.int32)

    def panel(which):
        block = lax.dynamic_slice_in_dim(matrix, which // col_devices * NB, NB, 1)
        return jnp.where(which % col_devices == my_col, block, 0.0)

    slab = lax.psum(jnp.concatenate([panel(target), panel(target + 1)], axis=1), "col")

    def top_rows(array):
        parts = []
        for at in (first, second):
            rows = lax.dynamic_slice_in_dim(array, at % height, NB, 0)
            parts.append(jnp.where(at // height == my_row, rows, 0.0))
        return parts

    below = jnp.where((global_row >= second)[:, None], slab, 0.0)
    gram = lax.dot_general(below, below, (((0,), (0,)), ((), ())), precision=HI)
    small = lax.psum(jnp.concatenate([gram] + top_rows(slab), axis=0), "row")
    product = lax.dot_general(below, matrix, (((0,), (0,)), ((), ())), precision=HI)
    bulk = jnp.concatenate([product] + top_rows(matrix), axis=0)
    bulk, small = lax.optimization_barrier((bulk, small))
    bulk = lax.psum(bulk, "row")
    factors = pl.pallas_call(
        factor_kernel,
        out_shape=jax.ShapeDtypeStruct((10, NB, NB), jnp.float32),
        in_specs=[pl.BlockSpec(memory_space=pltpu.VMEM)],
        out_specs=pl.BlockSpec(memory_space=pltpu.VMEM),
        scratch_shapes=[pltpu.VMEM((2, NB, NB), jnp.float32)] * 2,
        compiler_params=pltpu.CompilerParams(vmem_limit_bytes=16 * 1024 * 1024),
        cost_estimate=pl.CostEstimate(
            flops=10**9, bytes_accessed=100 * 10**6, transcendentals=0
        ),
    )(small)
    place1 = jnp.where(target % col_devices == my_col, target // col_devices, -1)
    place2 = jnp.where((target + 1) % col_devices == my_col, (target + 1) // col_devices, -1)
    scalars = jnp.stack(
        [
            my_row * height - first,
            place1,
            place2,
            target,
            my_col,
            jnp.int32(col_devices),
        ]
    ).astype(jnp.int32)
    return pl.pallas_call(
        finish_kernel,
        out_shape=jax.ShapeDtypeStruct((height, width), jnp.float32),
        in_specs=[pl.BlockSpec(memory_space=pltpu.SMEM)]
        + [pl.BlockSpec(memory_space=pltpu.VMEM)] * 4,
        out_specs=pl.BlockSpec(memory_space=pltpu.VMEM),
        compiler_params=pltpu.CompilerParams(vmem_limit_bytes=32 * 1024 * 1024),
    )(scalars, matrix, slab, bulk, factors)


def solution(mesh):
    return jax.shard_map(
        per_device,
        mesh=mesh,
        in_specs=(P("row", "col"), P()),
        out_specs=P("row", "col"),
        check_vma=False,
    )
```

time: 1960 us -> 198 us (0.10)
  other arithmetic: 732 us -> 6.19 us
  local copies, waits for them, and re-layouts: 649 us -> 2.73 us
  loops' own time: 240 us -> 0 us
  waiting for transfers between devices: 288 us -> 103 us
  Pallas kernels: 0 us -> 67.2 us
  matrix products: 24.3 us -> 4.39 us
    dynamic_slice x1280 -> x0, local copies, waits for them, and re-layouts: 648 us -> none  [the longest x512 301 us: upper_row_step(): pivot = lax.dynamic_index_in_dim(full_row, row_number, 0, keepdims=False)]
    div x512 -> x0, other arithmetic: 336 us -> none  [upper_row_step(): new_row = (unit_row - jnp.sum(off_part[:, None] * solved, axis=0)) / pivot]
    another operation x10 -> x0, loops' own time: 240 us -> none  [the longest x2 190 us: lower_cholesky(): return lax.fori_loop(0, order_size, column_step, start)[1]]
    psum x6 -> x3, waiting for transfers between devices: 288 us -> 103 us  [the longest x1 51.1 us: per_device(): small = lax.psum(jnp.concatenate([gram] + top_rows(slab), axis=0), 'row')]
    mul x768 -> x0, other arithmetic: 174 us -> none  [the longest x256 167 us: eliminate(): remaining = remaining - multiplier[:, None] * pivot_row[None, :]]
    add x1283 -> x0, other arithmetic: 126 us -> none  [the longest x768 65.1 us: place_row(): target_matrix + new_row[None, :] * (positions[:, None] == row_number).ast...]
    reduce_sum x770 -> x0, other arithmetic: 77 us -> none  [the longest x512 49.6 us: upper_row_step(): new_row = (unit_row - jnp.sum(off_part[:, None] * solved, axis=0)) / pivot]
    pallas_call x0 -> x2, Pallas kernels: none -> 67.2 us  [the longest x1 52.1 us: per_device(): pl.pallas_call(factor_kernel, out_shape=jax.ShapeDtypeStruct((10, NB, NB)...]
where the time goes in v1:
time: 198 us; the launch traced here: 197 us
  waiting for transfers between devices  103 us (52%)
  Pallas kernels  67.2 us (34%)
  between operations  14.1 us (7%)
  other arithmetic  6.19 us (3%)
  matrix products  4.39 us (2%)
  local copies, waits for them, and re-layouts  2.73 us (1%)
    pallas_call x1, Pallas kernels, per_device(): pl.pallas_call(factor_kernel, out_shape=jax.ShapeDtypeStruct((10, NB, NB)...  52.1 us
    psum x1, waiting for transfers between devices, per_device(): small = lax.psum(jnp.concatenate([gram] + top_rows(slab), axis=0), 'row')  51.1 us
    psum x1, waiting for transfers between devices, per_device(): lax.psum(jnp.concatenate([panel(target), panel(target + 1)], axis=1), 'col')  40.3 us
    pallas_call x1, Pallas kernels, per_device(): pl.pallas_call(finish_kernel, out_shape=jax.ShapeDtypeStruct((height, wid...  15 us
    psum x1, waiting for transfers between devices, per_device(): bulk = lax.psum(bulk, 'row')  11.3 us
  transfers between devices with their start and end apart: 3, of which 3 were waited for; matrix products, arithmetic and copies ran while one was open for 2% of the time, Pallas kernels for 26%

profile of v1, /device:TPU:0, one launch (start us, length us, event | category | flops | bytes accessed | tf_op | source)
XLA Modules:
  0.0 197.4 jit_solution(8484286601853386457)
XLA Ops:
  6.5 0.0 copy-start
  6.5 0.0 all-reduce.4.cloned.1.call-start
  7.4 1.1 dynamic-slice_select_fusion.3
  8.5 0.8 pad_maximum_fusion.1
  9.3 0.0 all-reduce.4.cloned.1.call-update
  9.4 0.0 all-reduce.6.cloned.1.call-start
  9.5 0.0 copy-done
  9.5 0.9 dynamic-slice_select_fusion.1
  10.4 40.3 %all-reduce.4.cloned.1.call-done.a_ref = f32[512,256]{1,0:T(8,128)} async-done(((f32[512,256]{1,0:T(8,128)}), f32[512,256]{1,0:T(8,128)}) %all-reduce.4.cloned.1.call-update) | async-done | bytes 524304 | tf_op jit(solution)/shard_map/psum | solution.py:149
  50.7 0.0 copy-start.1
  50.7 1.0 dynamic-slice_select_fusion.5
  51.8 2.4 %fusion = f32[256,256]{1,0:T(8,128)S(1)} fusion(f32[512,256]{1,0:T(8,128)} %all-reduce.4.cloned.1.call-done.a_ref, pred[512]{0:T(512)(128)(4,1)S(1)} %add_compare_fusion), kind=kOutput, calls=%fused_computation.5 | convolution fusion | flops 402784256 | bytes 786944 | tf_op jit(solution)/shard_map/dot_general | solution.py:159
  54.1 0.8 pad_maximum_fusion.2
  55.0 0.0 all-reduce.6.cloned.1.call-update
  55.0 0.0 all-reduce.8.cloned.1.call-start
  55.1 0.0 copy-done.1
  55.1 0.0 copy-start.4
  55.1 2.0 %fusion.2 = f32[256,1024]{1,0:T(8,128)S(1)} fusion(f32[512,1024]{1,0:T(8,128)S(1)} %copy-done, f32[512,256]{1,0:T(8,128)S(1)} %copy-done.1, pred[512]{0:T(512)(128)(4,1)S(1)} %add_compare_fusion), kind=kOutput, calls=%fused_computation.7 | convolution fusion | flops 1610743808 | bytes 3670528 | tf_op jit(solution)/shard_map/dot_general | solution.py:161
  57.1 0.0 copy-done.4
  57.1 1.5 pad_maximum_fusion
  58.6 51.1 %all-reduce.6.cloned.1.call-done.small_ref = f32[512,256]{1,0:T(8,128)} async-done(((f32[512,256]{1,0:T(8,128)}), f32[512,256]{1,0:T(8,128)}) %all-reduce.6.cloned.1.call-update) | async-done | bytes 524304 | tf_op jit(solution)/shard_map/psum | solution.py:160
  109.7 0.0 all-reduce.8.cloned.1.call-update
  109.8 0.1 stack.19.s_ref
  109.8 0.0 copy-start.3
  109.8 1.0 copy-done.3
  110.9 52.1 %shard_map.28.fac_ref = f32[10,128,128]{2,1,0:T(8,128)S(1)} custom-call(f32[512,256]{1,0:T(8,128)S(1)} %copy-done.3), custom_call_target="tpu_custom_call" | custom-call | flops 1000000000 | bytes 100000000 | tf_op jit(solution)/shard_map/pallas_call | solution.py:165
  163.0 11.3 %all-reduce.8.cloned.1.call-done.bulk_ref = f32[512,1024]{1,0:T(8,128)} async-done(((f32[512,1024]{1,0:T(8,128)}), f32[512,1024]{1,0:T(8,128)}) %all-reduce.8.cloned.1.call-update) | async-done | bytes 2097168 | tf_op jit(solution)/shard_map/psum | solution.py:164
  174.3 0.0 copy-start.2
  174.3 1.6 copy-done.2
  175.9 15.0 %shard_map.29 = f32[512,1024]{1,0:T(8,128)} custom-call(s32[6]{0:T(128)S(1)} %stack.19.s_ref, f32[512,1024]{1,0:T(8,128)S(1)} %copy-done, f32[512,256]{1,0:T(8,128)S(1)} %copy-done.1, f32[512,1024]{1,0:T(8,128)S(1)} %copy-done.2, f32[10,128,128]{2,1,0:T(8,128)S(1)} %shard_map.28.fac_ref), custom_call_target="tpu_custom_call" | custom-call | tf_op jit(solution)/shard_map/pallas_call | solution.py:188
  (1 shorter events, 0.0 us)
Async XLA Ops:
  6.5 3.0 %copy-start = (f32[512,1024]{1,0:T(8,128)S(1)}, f32[512,1024]{1,0:T(8,128)}, u32[]{:S(2)}) copy-start(f32[512,1024]{1,0:T(8,128)} %c_ref.1) | copy-start | bytes 6291460
  6.5 44.2 %all-reduce.4.cloned.1.call-start = ((), (), s32[]{:S(2)}) async-start(), calls=%async_computation | async-start | bytes 1048576 | tf_op jit(solution)/shard_map/psum | solution.py:149
  9.4 100.3 %all-reduce.6.cloned.1.call-start = ((), (), s32[]{:S(2)}) async-start(), calls=%async_computation.1 | async-start | bytes 1048576 | tf_op jit(solution)/shard_map/psum | solution.py:160
  50.7 4.3 %copy-start.1 = (f32[512,256]{1,0:T(8,128)S(1)}, f32[512,256]{1,0:T(8,128)}, u32[]{:S(2)}) copy-start(f32[512,256]{1,0:T(8,128)} %all-reduce.4.cloned.1.call-done.a_ref) | copy-start | bytes 1572868
  55.0 119.3 %all-reduce.8.cloned.1.call-start = ((), (), s32[]{:S(2)}) async-start(), calls=%async_computation.2 | async-start | bytes 4194304 | tf_op jit(solution)/shard_map/psum | solution.py:164
  55.1 2.0 %copy-start.4 = (f32[128,1024]{1,0:T(8,128)S(1)}, f32[128,1024]{1,0:T(8,128)}, u32[]{:S(2)}) copy-start(f32[128,1024]{1,0:T(8,128)} %get-tuple-element.10) | copy-start | bytes 1572868
  109.8 1.0 copy-start.3
  174.3 1.6 copy-start.2
Sparse Core Ops, SparseCore 0:
  9.7 40.9 all-reduce.3
  55.1 54.5 all-reduce.5
  113.3 60.9 all-reduce.7

commit v2 on v1

--- a/solution.py
+++ b/solution.py
@@ -85,6 +85,109 @@
         out_ref[i] = a
 
 
+def gather_kernel(block_ref, out_ref, slots, send_sem, recv_sem):
+    count = slots.shape[0]
+    me = lax.axis_index("col")
+    barrier = pltpu.get_barrier_semaphore()
+    for k in range(1, count):
+        pl.semaphore_signal(
+            barrier,
+            inc=1,
+            device_id={"col": lax.rem(me + k, count)},
+            device_id_type=pl.DeviceIdType.MESH,
+        )
+    pl.semaphore_wait(barrier, count - 1)
+    copies = []
+    for k in range(1, count):
+        copy = pltpu.make_async_remote_copy(
+            src_ref=block_ref,
+            dst_ref=slots.at[me],
+            send_sem=send_sem.at[k],
+            recv_sem=recv_sem.at[k],
+            device_id={"col": lax.rem(me + k, count)},
+            device_id_type=pl.DeviceIdType.MESH,
+        )
+        copy.start()
+        copies.append(copy)
+    slots[me] = block_ref[...]
+    for copy in copies:
+        copy.wait_recv()
+    out_ref[...] = slots[...]
+    for copy in copies:
+        copy.wait_send()
+
+
+def prepare_kernel(s_ref, slots_ref, c_ref, slab_ref, part_ref, bulk_ref):
+    height, width = c_ref.shape
+    rel = lax.broadcasted_iota(jnp.int32, (height, 2 * NB), 0) + s_ref[0]
+    slab_ref[:, 0:NB] = slots_ref[s_ref[5]]
+    slab_ref[:, NB:] = slots_ref[s_ref[6]]
+    below = jnp.where(rel >= NB, slab_ref[...], 0.0)
+    part_ref[0 : 2 * NB, :] = mm(below, below, 0, 0)
+    below_t = below.T
+    step = 2 * NB
+
+    def column(i, _):
+        at = pl.ds(pl.multiple_of(i * step, step), step)
+        bulk_ref[0 : 2 * NB, at] = mm(below_t, c_ref[:, at])
+        return 0
+
+    lax.fori_loop(0, width // step, column, 0)
+    for i in range(2):
+        at = pl.ds(pl.multiple_of(s_ref[1 + i], NB), NB)
+        put = slice((2 + i) * NB, (3 + i) * NB)
+        here = s_ref[3 + i] > 0
+        part_ref[put, :] = jnp.where(here, slab_ref[at, :], 0.0)
+        bulk_ref[put, :] = jnp.where(here, c_ref[at, :], 0.0)
+
+
+def small_kernel(part, out_ref, arrived, total, send_sem, recv_sem, send_sem2, recv_sem2):
+    count = arrived.shape[0]
+    chunk = arrived.shape[1]
+    me = lax.axis_index("row")
+    peers = [lax.rem(me + k, count) for k in range(count)]
+    barrier = pltpu.get_barrier_semaphore()
+    for k in range(1, count):
+        pl.semaphore_signal(
+            barrier, inc=1, device_id={"row": peers[k]}, device_id_type=pl.DeviceIdType.MESH
+        )
+    pl.semaphore_wait(barrier, count - 1)
+
+    def send(src, dst, k, sems):
+        copy = pltpu.make_async_remote_copy(
+            src_ref=src,
+            dst_ref=dst,
+            send_sem=sems[0].at[k],
+            recv_sem=sems[1].at[k],
+            device_id={"row": peers[k]},
+            device_id_type=pl.DeviceIdType.MESH,
+        )
+        copy.start()
+        return copy
+
+    def rows_of(device):
+        return pl.ds(pl.multiple_of(device * chunk, chunk), chunk)
+
+    mine = rows_of(me)
+    copies = [
+        send(part.at[rows_of(peers[k])], arrived.at[k], k, (send_sem, recv_sem))
+        for k in range(1, count)
+    ]
+    value = part[mine, :]
+    for k in range(1, count):
+        copies[k - 1].wait_recv()
+        value = value + arrived[k]
+    total[mine, :] = value
+    again = [
+        send(total.at[mine], total.at[mine], k, (send_sem2, recv_sem2)) for k in range(1, count)
+    ]
+    for copy in again:
+        copy.wait_recv()
+    out_ref[...] = total[...]
+    for copy in copies + again:
+        copy.wait_send()
+
+
 def finish_kernel(s_ref, c_ref, a_ref, bulk_ref, fac_ref, out_ref):
     row_off = s_ref[0]
     place1, place2, target, my_col, col_devices = s_ref[1], s_ref[2], s_ref[3], s_ref[4], s_ref[5]
@@ -140,28 +243,64 @@
     target = panel_index[0]
     first = target * NB
     second = first + NB
-    global_row = my_row * height + jnp.arange(height, dtype=jnp.int32)
-
-    def panel(which):
-        block = lax.dynamic_slice_in_dim(matrix, which // col_devices * NB, NB, 1)
-        return jnp.where(which % col_devices == my_col, block, 0.0)
-
-    slab = lax.psum(jnp.concatenate([panel(target), panel(target + 1)], axis=1), "col")
-
-    def top_rows(array):
-        parts = []
-        for at in (first, second):
-            rows = lax.dynamic_slice_in_dim(array, at % height, NB, 0)
-            parts.append(jnp.where(at // height == my_row, rows, 0.0))
-        return parts
-
-    below = jnp.where((global_row >= second)[:, None], slab, 0.0)
-    gram = lax.dot_general(below, below, (((0,), (0,)), ((), ())), precision=HI)
-    small = lax.psum(jnp.concatenate([gram] + top_rows(slab), axis=0), "row")
-    product = lax.dot_general(below, matrix, (((0,), (0,)), ((), ())), precision=HI)
-    bulk = jnp.concatenate([product] + top_rows(matrix), axis=0)
-    bulk, small = lax.optimization_barrier((bulk, small))
+
+    vmem = pl.BlockSpec(memory_space=pltpu.VMEM)
+    smem = pl.BlockSpec(memory_space=pltpu.SMEM)
+    owners = jnp.stack([target % col_devices, (target + 1) % col_devices]).astype(jnp.int32)
+    held = jnp.where(owners[1] == my_col, target + 1, target) // col_devices
+    candidate = lax.dynamic_slice_in_dim(matrix, held * NB, NB, 1)
+    row_devices = lax.axis_size("row")
+    chunk = 4 * NB // row_devices
+    slots = pl.pallas_call(
+        gather_kernel,
+        out_shape=jax.ShapeDtypeStruct((col_devices, height, NB), jnp.float32),
+        in_specs=[vmem],
+        out_specs=vmem,
+        scratch_shapes=[
+            pltpu.VMEM((col_devices, height, NB), jnp.float32),
+            pltpu.SemaphoreType.DMA((col_devices,)),
+            pltpu.SemaphoreType.DMA((col_devices,)),
+        ],
+        compiler_params=pltpu.CompilerParams(
+            collective_id=0, has_side_effects=True, vmem_limit_bytes=24 * 1024 * 1024
+        ),
+    )(candidate)
+    tops = [first, second]
+    places = jnp.stack(
+        [my_row * height - first]
+        + [at % height for at in tops]
+        + [(at // height == my_row).astype(jnp.int32) for at in tops]
+        + [owners[0], owners[1]]
+    ).astype(jnp.int32)
+    slab, part, bulk = pl.pallas_call(
+        prepare_kernel,
+        out_shape=[
+            jax.ShapeDtypeStruct((height, 2 * NB), jnp.float32),
+            jax.ShapeDtypeStruct((4 * NB, 2 * NB), jnp.float32),
+            jax.ShapeDtypeStruct((4 * NB, width), jnp.float32),
+        ],
+        in_specs=[smem, vmem, vmem],
+        out_specs=[vmem] * 3,
+        compiler_params=pltpu.CompilerParams(vmem_limit_bytes=32 * 1024 * 1024),
+    )(places, slots, matrix)
     bulk = lax.psum(bulk, "row")
+    small = pl.pallas_call(
+        small_kernel,
+        out_shape=jax.ShapeDtypeStruct((4 * NB, 2 * NB), jnp.float32),
+        in_specs=[vmem],
+        out_specs=vmem,
+        scratch_shapes=[
+            pltpu.VMEM((row_devices, chunk, 2 * NB), jnp.float32),
+            pltpu.VMEM((4 * NB, 2 * NB), jnp.float32),
+        ]
+        + [pltpu.SemaphoreType.DMA((row_devices,))] * 4,
+        compiler_params=pltpu.CompilerParams(
+            collective_id=1, has_side_effects=True, vmem_limit_bytes=16 * 1024 * 1024
+        ),
+        cost_estimate=pl.CostEstimate(
+            flops=10**8, bytes_accessed=30 * 10**6, transcendentals=0
+        ),
+    )(part)
     factors = pl.pallas_call(
         factor_kernel,
         out_shape=jax.ShapeDtypeStruct((10, NB, NB), jnp.float32),

time: 198 us -> 142 us (0.72)
  the two profiles are of different devices: /device:TPU:0 before, /device:TPU:9 now
where the time goes in v2:
time: 142 us
  Pallas kernels  123 us (87%)
  between operations  14.3 us (10%)
  local copies, waits for them, and re-layouts  4.33 us (3%)
    pallas_call x1, Pallas kernels, per_device(): pl.pallas_call(factor_kernel, out_shape=jax.ShapeDtypeStruct((10, NB, NB)...  52.1 us
    pallas_call x1, Pallas kernels, per_device(): pl.pallas_call(gather_kernel, out_shape=jax.ShapeDtypeStruct((col_devices...  26.3 us
    pallas_call x1, Pallas kernels, per_device(): pl.pallas_call(small_kernel, out_shape=jax.ShapeDtypeStruct((4 * NB, 2 *...  24.3 us
    pallas_call x1, Pallas kernels, per_device(): pl.pallas_call(finish_kernel, out_shape=jax.ShapeDtypeStruct((height, wid...  15 us
    pallas_call x1, Pallas kernels, per_device(): pl.pallas_call(prepare_kernel, out_shape=[jax.ShapeDtypeStruct((height, 2...  5.14 us
    unnamed x6, local copies, waits for them, and re-layouts  3.18 us
  transfers between devices with their start and end apart: 1, of which 0 were waited for; matrix products, arithmetic and copies ran while one was open for 0% of the time, Pallas kernels for 54%

profile of v2, /device:TPU:9, one launch (start us, length us, event | category | flops | bytes accessed | tf_op | source)
XLA Modules:
  0.0 141.5 jit_solution(2133398648200275047)
XLA Ops:
  6.5 0.0 all-reduce.2.cloned.1.call-start
  7.3 1.0 constant_dynamic-slice_fusion.block_ref
  8.3 26.3 %shard_map.28.slots_ref = f32[4,512,128]{2,1,0:T(8,128)S(1)} custom-call(f32[512,128]{1,0:T(8,128)S(1)} %constant_dynamic-slice_fusion.block_ref), custom_call_target="tpu_custom_call" | custom-call | tf_op jit(solution)/shard_map/pallas_call | solution.py:254
  34.6 0.1 stack.56.s_ref
  34.7 0.0 copy-start
  34.7 1.6 %copy-done = f32[512,1024]{1,0:T(8,128)S(1)} copy-done((f32[512,1024]{1,0:T(8,128)S(1)}, f32[512,1024]{1,0:T(8,128)}, u32[]{:S(2)}) %copy-start) | copy-done | bytes 2097176
  36.3 5.1 %shard_map.29 = (f32[512,256]{1,0:T(8,128)S(1)}, f32[512,256]{1,0:T(8,128)S(1)}, f32[512,1024]{1,0:T(8,128)}) custom-call(s32[7]{0:T(128)S(1)} %stack.56.s_ref, f32[4,512,128]{2,1,0:T(8,128)S(1)} %shard_map.28.slots_ref, f32[512,1024]{1,0:T(8,128)S(1)} %copy-done), custom_call_target="tpu_custom_call" | custom-call | tf_op jit(solution)/shard_map/pallas_call | solution.py:275
  41.5 0.0 all-reduce.2.cloned.1.call-update
  41.5 0.1 stack.47.s_ref
  41.6 24.3 %shard_map.30.small_ref = f32[512,256]{1,0:T(8,128)S(1)} custom-call(f32[512,256]{1,0:T(8,128)S(1)} %get-tuple-element.10.part), custom_call_target="tpu_custom_call" | custom-call | flops 100000000 | bytes 30000000 | tf_op jit(solution)/shard_map/pallas_call | solution.py:287
  65.9 0.0 copy-start.1
  65.9 52.1 %shard_map.31.fac_ref = f32[10,128,128]{2,1,0:T(8,128)S(1)} custom-call(f32[512,256]{1,0:T(8,128)S(1)} %shard_map.30.small_ref), custom_call_target="tpu_custom_call" | custom-call | flops 1000000000 | bytes 100000000 | tf_op jit(solution)/shard_map/pallas_call | solution.py:304
  118.0 0.0 all-reduce.2.cloned.1.call-done.bulk_ref
  118.0 0.0 copy-done.1
  118.1 0.0 copy-start.2
  118.1 1.6 %copy-done.2 = f32[512,1024]{1,0:T(8,128)S(1)} copy-done((f32[512,1024]{1,0:T(8,128)S(1)}, f32[512,1024]{1,0:T(8,128)}, u32[]{:S(2)}) %copy-start.2) | copy-done | bytes 2097176
  119.6 15.0 %shard_map.32 = f32[512,1024]{1,0:T(8,128)} custom-call(s32[6]{0:T(128)S(1)} %stack.47.s_ref, f32[512,1024]{1,0:T(8,128)S(1)} %copy-done.1, f32[512,256]{1,0:T(8,128)S(1)} %get-tuple-element.8.a_ref, f32[512,1024]{1,0:T(8,128)S(1)} %copy-done.2, f32[10,128,128]{2,1,0:T(8,128)S(1)} %shard_map.31.fac_ref), custom_call_target="tpu_custom_call" | custom-call | tf_op jit(solution)/shard_map/pallas_call | solution.py:327
Async XLA Ops:
  6.5 111.5 %all-reduce.2.cloned.1.call-start = ((), (), s32[]{:S(2)}) async-start(), calls=%async_computation | async-start | bytes 4194304 | tf_op jit(solution)/shard_map/psum | solution.py:286
  34.7 1.6 %copy-start = (f32[512,1024]{1,0:T(8,128)S(1)}, f32[512,1024]{1,0:T(8,128)}, u32[]{:S(2)}) copy-start(f32[512,1024]{1,0:T(8,128)} %c_ref.3) | copy-start | bytes 6291460
  65.9 52.1 %copy-start.1 = (f32[512,1024]{1,0:T(8,128)S(1)}, f32[512,1024]{1,0:T(8,128)}, u32[]{:S(2)}) copy-start(f32[512,1024]{1,0:T(8,128)} %c_ref.3) | copy-start | bytes 6291460
  118.1 1.6 %copy-start.2 = (f32[512,1024]{1,0:T(8,128)S(1)}, f32[512,1024]{1,0:T(8,128)}, u32[]{:S(2)}) copy-start(f32[512,1024]{1,0:T(8,128)} %all-reduce.2.cloned.1.call-done.bulk_ref) | copy-start | bytes 6291460
Sparse Core Ops, SparseCore 0:
  41.6 68.2 all-reduce.1

commit v3 on v2

--- a/solution.py
+++ b/solution.py
@@ -7,6 +7,7 @@
 
 NB = 128
 SUB = 32
+GROUP = 4
 HI = lax.Precision.HIGHEST
 
 
@@ -21,7 +22,7 @@
     rows = lax.broadcasted_iota(jnp.int32, (NB, NB), 0)
     cols = lax.broadcasted_iota(jnp.int32, (NB, NB), 1)
     unit = (rows == cols).astype(jnp.float32)
-    sub_row = lax.broadcasted_iota(jnp.int32, (SUB, 1), 0)
+    sub_row = lax.broadcasted_iota(jnp.int32, (SUB, NB), 0)
     for i, a in enumerate(chains):
         m_ref[i] = a
         n_ref[i] = unit
@@ -29,14 +30,23 @@
     for start in range(0, NB, SUB):
         m = [m_ref[i, start : start + SUB, :] for i in range(count)]
         n = [n_ref[i, start : start + SUB, :] for i in range(count)]
-        inv = [jnp.zeros((SUB, 1), jnp.float32) for _ in range(count)]
-        for j in range(SUB):
-            c = start + j
-            for i in range(count):
-                recip = 1.0 / m[i][j : j + 1, c : c + 1]
-                inv[i] = jnp.where(sub_row == j, recip, inv[i])
-                if j < SUB - 1:
-                    mult = jnp.where(sub_row > j, m[i][:, c : c + 1] * recip, 0.0)
+        inv = [jnp.zeros((SUB, NB), jnp.float32) for _ in range(count)]
+        for j0 in range(0, SUB, GROUP):
+            spread = [
+                [
+                    jnp.broadcast_to(m[i][:, start + j : start + j + 1], (SUB, NB))
+                    for j in range(j0, j0 + GROUP)
+                ]
+                for i in range(count)
+            ]
+            for g in range(GROUP):
+                j = j0 + g
+                for i in range(count):
+                    recip = 1.0 / spread[i][g][j : j + 1, :]
+                    inv[i] = jnp.where(sub_row == j, recip, inv[i])
+                    mult = jnp.where(sub_row > j, spread[i][g] * recip, 0.0)
+                    for k in range(g + 1, GROUP):
+                        spread[i][k] = spread[i][k] - mult * spread[i][k][j : j + 1, :]
                     m[i] = m[i] - mult * m[i][j : j + 1, :]
                     n[i] = n[i] - mult * n[i][j : j + 1, :]
         for i in range(count):
@@ -222,7 +232,7 @@
         out_ref[:, at] = c_ref[:, at] - mm(both, jnp.concatenate([x1, x2], axis=0))
         return 0
 
-    lax.fori_loop(0, width // step, column, 0)
+    lax.fori_loop(0, width // step, column, 0, unroll=True)
 
     @pl.when(place1 >= 0)
     def _():

time: 142 us -> 133 us (0.937)
  the two profiles are of different devices: /device:TPU:9 before, /device:TPU:0 now
where the time goes in v3:
time: 133 us
  Pallas kernels  87.4 us (66%)
  waiting for transfers between devices  26.7 us (20%)
  between operations  14.3 us (11%)
  local copies, waits for them, and re-layouts  4.34 us (3%)
    pallas_call x1, Pallas kernels, per_device(): pl.pallas_call(factor_kernel, out_shape=jax.ShapeDtypeStruct((10, NB, NB)...  27.6 us
    psum x1, waiting for transfers between devices, per_device(): bulk = lax.psum(bulk, 'row')  26.7 us
    pallas_call x1, Pallas kernels, per_device(): pl.pallas_call(gather_kernel, out_shape=jax.ShapeDtypeStruct((col_devices...  23.1 us
    pallas_call x1, Pallas kernels, per_device(): pl.pallas_call(small_kernel, out_shape=jax.ShapeDtypeStruct((4 * NB, 2 *...  19.3 us
    pallas_call x1, Pallas kernels, per_device(): pl.pallas_call(finish_kernel, out_shape=jax.ShapeDtypeStruct((height, wid...  12.3 us
    pallas_call x1, Pallas kernels, per_device(): pl.pallas_call(prepare_kernel, out_shape=[jax.ShapeDtypeStruct((height, 2...  5.13 us
    unnamed x6, local copies, waits for them, and re-layouts  3.19 us
  transfers between devices with their start and end apart: 1, of which 1 were waited for; matrix products, arithmetic and copies ran while one was open for 0% of the time, Pallas kernels for 35%

profile of v3, /device:TPU:0, one launch (start us, length us, event | category | flops | bytes accessed | tf_op | source)
XLA Modules:
  0.0 132.8 jit_solution(13108824269211720691)
XLA Ops:
  6.5 0.0 all-reduce.2.cloned.1.call-start
  7.3 1.0 constant_dynamic-slice_fusion.block_ref
  8.3 23.1 %shard_map.28.slots_ref = f32[4,512,128]{2,1,0:T(8,128)S(1)} custom-call(f32[512,128]{1,0:T(8,128)S(1)} %constant_dynamic-slice_fusion.block_ref), custom_call_target="tpu_custom_call" | custom-call | tf_op jit(solution)/shard_map/pallas_call | solution.py:264
  31.4 0.1 stack.56.s_ref
  31.5 0.0 copy-start
  31.5 1.6 %copy-done = f32[512,1024]{1,0:T(8,128)S(1)} copy-done((f32[512,1024]{1,0:T(8,128)S(1)}, f32[512,1024]{1,0:T(8,128)}, u32[]{:S(2)}) %copy-start) | copy-done | bytes 2097176
  33.1 5.1 %shard_map.29 = (f32[512,256]{1,0:T(8,128)S(1)}, f32[512,256]{1,0:T(8,128)S(1)}, f32[512,1024]{1,0:T(8,128)}) custom-call(s32[7]{0:T(128)S(1)} %stack.56.s_ref, f32[4,512,128]{2,1,0:T(8,128)S(1)} %shard_map.28.slots_ref, f32[512,1024]{1,0:T(8,128)S(1)} %copy-done), custom_call_target="tpu_custom_call" | custom-call | tf_op jit(solution)/shard_map/pallas_call | solution.py:285
  38.2 0.0 all-reduce.2.cloned.1.call-update
  38.3 0.1 stack.47.s_ref
  38.4 19.3 %shard_map.30.small_ref = f32[512,256]{1,0:T(8,128)S(1)} custom-call(f32[512,256]{1,0:T(8,128)S(1)} %get-tuple-element.10.part), custom_call_target="tpu_custom_call" | custom-call | flops 100000000 | bytes 30000000 | tf_op jit(solution)/shard_map/pallas_call | solution.py:297
  57.7 0.0 copy-start.1
  57.7 27.6 %shard_map.31.fac_ref = f32[10,128,128]{2,1,0:T(8,128)S(1)} custom-call(f32[512,256]{1,0:T(8,128)S(1)} %shard_map.30.small_ref), custom_call_target="tpu_custom_call" | custom-call | flops 1000000000 | bytes 100000000 | tf_op jit(solution)/shard_map/pallas_call | solution.py:314
  85.3 26.7 %all-reduce.2.cloned.1.call-done.bulk_ref = f32[512,1024]{1,0:T(8,128)} async-done(((f32[512,1024]{1,0:T(8,128)}), f32[512,1024]{1,0:T(8,128)}) %all-reduce.2.cloned.1.call-update) | async-done | bytes 2097168 | tf_op jit(solution)/shard_map/psum | solution.py:296
  112.0 0.0 copy-done.1
  112.0 0.0 copy-start.2
  112.0 1.6 %copy-done.2 = f32[512,1024]{1,0:T(8,128)S(1)} copy-done((f32[512,1024]{1,0:T(8,128)S(1)}, f32[512,1024]{1,0:T(8,128)}, u32[]{:S(2)}) %copy-start.2) | copy-done | bytes 2097176
  113.6 12.3 %shard_map.32 = f32[512,1024]{1,0:T(8,128)} custom-call(s32[6]{0:T(128)S(1)} %stack.47.s_ref, f32[512,1024]{1,0:T(8,128)S(1)} %copy-done.1, f32[512,256]{1,0:T(8,128)S(1)} %get-tuple-element.8.a_ref, f32[512,1024]{1,0:T(8,128)S(1)} %copy-done.2, f32[10,128,128]{2,1,0:T(8,128)S(1)} %shard_map.31.fac_ref), custom_call_target="tpu_custom_call" | custom-call | tf_op jit(solution)/shard_map/pallas_call | solution.py:337
Async XLA Ops:
  6.5 105.5 %all-reduce.2.cloned.1.call-start = ((), (), s32[]{:S(2)}) async-start(), calls=%async_computation | async-start | bytes 4194304 | tf_op jit(solution)/shard_map/psum | solution.py:296
  31.5 1.6 %copy-start = (f32[512,1024]{1,0:T(8,128)S(1)}, f32[512,1024]{1,0:T(8,128)}, u32[]{:S(2)}) copy-start(f32[512,1024]{1,0:T(8,128)} %c_ref.3) | copy-start | bytes 6291460
  57.7 54.3 %copy-start.1 = (f32[512,1024]{1,0:T(8,128)S(1)}, f32[512,1024]{1,0:T(8,128)}, u32[]{:S(2)}) copy-start(f32[512,1024]{1,0:T(8,128)} %c_ref.3) | copy-start | bytes 6291460
  112.0 1.6 %copy-start.2 = (f32[512,1024]{1,0:T(8,128)S(1)}, f32[512,1024]{1,0:T(8,128)}, u32[]{:S(2)}) copy-start(f32[512,1024]{1,0:T(8,128)} %all-reduce.2.cloned.1.call-done.bulk_ref) | copy-start | bytes 6291460
Sparse Core Ops, SparseCore 0:
  38.4 73.5 all-reduce.1
